TPU v7x, 128 devices: a whole 4x4x4 slice. The times are simulated.
128 devices in a mesh: space: 64 (over z, x, y_lo, core), samp: 2 (over y_hi).
Axes of the slice: x: 4, y: 4 (y_hi: 2, y_lo: 2; y = y_hi * 2 + y_lo), z: 4, core: 2. Of those that a mesh axis runs over, the one named last changes fastest.
Arguments:
- features: bfloat16 [2, 32, 128, 128, 128], P('samp', None, 'space'), may hold values from -6 to 6
- pre_act: bfloat16 [2, 32, 128, 128, 128], P('samp', None, 'space'), may hold values from -8 to 8
- cotangent: bfloat16 [2, 32, 128, 128, 128], P('samp', None, 'space'), may hold values from -6 to 6
- mix_weight: bfloat16 [32, 32], replicated, may hold values from -1 to 1
- spec_weight: float32 [2, 32, 1024, 32, 32], P(None, None, 'space'), may hold values from -3 to 3
Outputs:
- grad_field: bfloat16 [2, 32, 128, 128, 128], P('samp', None, 'space')
- grad_spec: float32 [2, 32, 1024, 32, 32], P(None, None, ('space', 'samp'))
All inputs are finite; a program needn't handle non-finite values.
Results may differ from a plain program's by a relative error of at most 0.0052.
Values sent between devices are 32-bit elements; how exact they have to be, the bound alone decides.
A program may use at most 576 MiB of HBM per device.

v0:
```python
import functools
import math

import jax
import jax.numpy as jnp
import ml_dtypes
import numpy as np
from jax import lax
from jax.experimental import pallas as pl
from jax.experimental.pallas import tpu as pltpu
from jax.sharding import PartitionSpec as P

MESH = pl.DeviceIdType.MESH
BF = jnp.bfloat16
F32 = jnp.float32
C = 32
M = 32
G = 128
NX = 128
NDEV = 128
NRM = 1.0 / math.sqrt(NX * G * G)


def split_np(values):
    high = values.astype(ml_dtypes.bfloat16)
    low = (values - high.astype(np.float64)).astype(ml_dtypes.bfloat16)
    return high, low


def tables():
    freq = np.arange(M) - M // 2
    pos = np.arange(G)

    def waves(positions, freqs):
        angles = np.mod(positions[:, None] * freqs[None, :], G) * (2.0 * math.pi / G)
        return np.cos(angles), np.sin(angles)

    cos_z, sin_z = waves(pos, np.arange(M))
    cos_c, sin_c = waves(pos, freq)
    cz = cos_z.reshape(G, 4, 8)
    sz = sin_z.reshape(G, 4, 8)
    wz = np.zeros((2, G, 2, 4, 2, 2, 8))
    for x in range(2):
        wz[x, :, 0, :, x, 0] = cz
        wz[x, :, 0, :, x, 1] = -sz
        wz[x, :, 1, :, x, 0] = -sz
        wz[x, :, 1, :, x, 1] = -cz
    wz = wz.reshape(256, 256).astype(ml_dtypes.bfloat16)
    ty = np.concatenate([cos_c.T, sin_c.T], axis=1)
    ty = np.concatenate(split_np(ty), axis=0)
    tx = np.zeros((2, M, NX, 2))
    tx[0, :, :, 0] = cos_c.T
    tx[0, :, :, 1] = sin_c.T
    tx[1, :, :, 0] = -sin_c.T
    tx[1, :, :, 1] = cos_c.T
    tx = tx.reshape(64, 256)
    txh = np.concatenate(split_np(tx * NRM), axis=0)
    xh, xl = split_np(tx.T.copy())
    xs = np.concatenate([xh, xh, xl], axis=1)
    ys = np.zeros((2, G, 2, M))
    ys[0, :, 0] = cos_c
    ys[0, :, 1] = -sin_c
    ys[1, :, 0] = sin_c
    ys[1, :, 1] = cos_c
    yh, yl = split_np(ys.reshape(256, 64) * NRM)
    ys = np.concatenate([yh, yh, yl], axis=1)
    zs = np.zeros((2, 4, 8, 4, 4, G))
    ck = cos_z.T.reshape(8, 4, G).transpose(1, 0, 2)
    sk = sin_z.T.reshape(8, 4, G).transpose(1, 0, 2)
    for i in range(4):
        zs[0, :, :, i, i] = ck
        zs[1, :, :, i, i] = -sk
    zh, zl = split_np(zs.reshape(256, 512))
    eye8 = np.eye(8)
    spread = np.broadcast_to(eye8[None, :, :, None], (C, 8, 8, C)).reshape(256, 256)
    order = np.einsum("cd,kl->ckld", np.eye(C), eye8).reshape(256, 256)
    rep = np.repeat(np.eye(C), 16, axis=0)
    names = dict(wz=wz, ty=ty, tx=txh, xs=xs, ys=ys, zh=zh, zl=zl, spread=spread, order=order, rep=rep)
    return {name: np.ascontiguousarray(v).astype(ml_dtypes.bfloat16) for name, v in names.items()}


def halves(values):
    high = values.astype(BF)
    return high, (values - high.astype(F32)).astype(BF)


def dot(left, right):
    return jnp.dot(left, right, preferred_element_type=F32)


def gelu_slope(values):
    return 0.5 * (1.0 + lax.erf(values * 0.7071067811865476)) + values * (
        jnp.exp(-0.5 * values * values) * 0.3989422804014327
    )


def exchange_lanes(tiles, unit, lane):
    tiles = list(tiles)
    step = 1
    while step < len(tiles):
        keep = (lane // (unit * step)) % 2 == 0
        for i in range(len(tiles)):
            if i & step:
                continue
            low, high = tiles[i], tiles[i | step]
            tiles[i] = jnp.where(keep, low, pltpu.roll(high, unit * step, 1))
            tiles[i | step] = jnp.where(keep, pltpu.roll(low, 128 - unit * step, 1), high)
        step *= 2
    return tiles


def kernel(
    feat_hbm, pre_hbm, cot_hbm, mix_ref, spec_hbm,
    wz, ty, tx, xs, ys, zh, zl, spread, order, rep,
    field_hbm, grad_hbm,
    feat, pre, cot, wraw, up, wpack, ysc, sh, su, rh, ru, sr, rr, hx, gpack, gout, mixed, kron, fout,
    in_sems, h_sems, u_sems, r_sems, out_sems,
):
    space = lax.axis_index("space")
    samp = lax.axis_index("samp")
    me = space * 2 + samp
    slot = samp * 64 + space
    quarter = lax.rem(me, 4)

    copy_pre = pltpu.make_async_copy(pre_hbm, pre, in_sems.at[0])
    copy_cot = pltpu.make_async_copy(cot_hbm, cot, in_sems.at[1])
    copy_feat = pltpu.make_async_copy(feat_hbm, feat, in_sems.at[2])
    copy_spec = pltpu.make_async_copy(
        spec_hbm.at[:, pl.ds(samp * 256, 256), :], wraw, in_sems.at[3]
    )
    copy_pre.start()
    copy_cot.start()
    copy_feat.start()
    copy_spec.start()

    def device(d):
        return (lax.div(d, 2), lax.rem(d, 2))

    barrier = pltpu.get_barrier_semaphore()

    def greet(j, carry):
        d = lax.rem(me + j, NDEV)
        pl.semaphore_signal(barrier, inc=1, device_id=device(d), device_id_type=MESH)
        return carry

    lax.fori_loop(1, NDEV, greet, 0)

    lane8 = lax.broadcasted_iota(jnp.int32, (8, 128), 1)

    def spectra(source, half, out):
        def pair(cp, carry):
            c0 = half * 16 + cp * 2
            z0 = dot(jnp.concatenate([source[c0, 0], source[c0, 1]], axis=1), wz[...])
            z1 = dot(jnp.concatenate([source[c0 + 1, 0], source[c0 + 1, 1]], axis=1), wz[...])
            r = jnp.concatenate(
                [
                    jnp.concatenate([z0[:, :128], z1[:, :128]], axis=1),
                    jnp.concatenate([z0[:, 128:], z1[:, 128:]], axis=1),
                ],
                axis=0,
            )
            high, low = halves(r)
            p = dot(ty[...], high)
            y = p[:32] + p[32:] + dot(ty[0:32, :], low)
            ysc[cp * 2] = y[:, :128]
            ysc[cp * 2 + 1] = y[:, 128:]
            return carry

        lax.fori_loop(0, 8, pair, 0)
        for bo in range(4):
            tiles = [ysc[c, bo * 8 : bo * 8 + 8, :] for c in range(16)]
            tiles = exchange_lanes(tiles, 8, lane8)
            for n in range(16):
                q, xr = n // 4, n % 4
                out[pl.ds(bo * 256 + q * 8 + xr * 2 + half, 8, stride=32), :] = tiles[n]

    def send_all(src, src_at, dst, dst_at, sems, keep_sem):
        def send(j, carry):
            d = lax.rem(me + j, NDEV)
            pltpu.make_async_remote_copy(
                src_ref=src.at[pl.ds(pl.multiple_of(src_at(d) * 8, 8), 8), :],
                dst_ref=dst.at[pl.ds(pl.multiple_of(dst_at * 8, 8), 8), :],
                send_sem=sems.at[0],
                recv_sem=sems.at[1],
                device_id=device(d),
                device_id_type=MESH,
            ).start()
            return carry

        lax.fori_loop(1, NDEV, send, 0)
        own = pltpu.make_async_copy(
            src.at[pl.ds(pl.multiple_of(src_at(me) * 8, 8), 8), :],
            dst.at[pl.ds(pl.multiple_of(dst_at * 8, 8), 8), :],
            keep_sem,
        )
        own.start()
        return own

    def arrived(ref, sem):
        part = ref.at[pl.ds(0, (NDEV - 1) * 8), :]
        pltpu.make_async_copy(part, part, sem).wait()

    copy_pre.wait()
    copy_cot.wait()

    def slope(c, carry):
        for x in range(2):
            values = cot[c, x].astype(F32) * gelu_slope(pre[c, x].astype(F32))
            up[c, x] = values.astype(BF)
        return carry

    lax.fori_loop(0, C, slope, 0)
    for half in range(2):
        spectra(up, half, sh)
    pl.semaphore_wait(barrier, NDEV - 1)
    own_h = send_all(sh, lambda d: d, rh, slot, h_sems, h_sems.at[2])

    copy_feat.wait()
    for half in range(2):
        spectra(feat, half, su)
    own_u = send_all(su, lambda d: d, ru, slot, u_sems, u_sems.at[2])

    copy_spec.wait()

    def pack(a, carry):
        for ri in range(2):
            for j in range(2):
                parts = [
                    wraw[ri * 32 + a, pl.ds((j * 4 + k) * 32, 32), :] for k in range(4)
                ]
                wpack[ri * 2 + j, pl.ds(a, 32, stride=32), :] = jnp.concatenate(parts, axis=1)
        return carry

    lax.fori_loop(0, M, pack, 0)

    turned = lax.dot_general(
        rep[...], mix_ref[...], (((1,), (1,)), ((), ())), preferred_element_type=F32
    ).astype(BF)
    wide = lax.dot_general(
        turned, rep[...], (((1,), (1,)), ((), ())), preferred_element_type=F32
    )
    row = lax.broadcasted_iota(jnp.int32, (512, 512), 0)
    col = lax.broadcasted_iota(jnp.int32, (512, 512), 1)
    kron[...] = jnp.where(lax.rem(row, 16) == lax.rem(col, 16), wide, 0.0).astype(BF)

    def mixing(yb, carry):
        y0 = pl.multiple_of(yb * 16, 16)
        for x in range(2):
            block = up[:, x, pl.ds(y0, 16), :].reshape(512, 128)
            mixed[:, x, pl.ds(y0, 16), :] = dot(kron[...], block).reshape(C, 16, 128)
        return carry

    lax.fori_loop(0, 8, mixing, 0)

    def x_sums(ref, t):
        r = jnp.concatenate(
            [ref[pl.ds(t * 512, 256, stride=2), :], ref[pl.ds(t * 512 + 1, 256, stride=2), :]],
            axis=1,
        )
        high, low = halves(r)
        p = dot(tx[...], high)
        return p[:64] + p[64:] + dot(tx[0:64, :], low)

    arrived(rh, h_sems.at[1])
    own_h.wait()
    lane256 = lax.broadcasted_iota(jnp.int32, (1, 256), 1)
    single = jnp.logical_and(lax.rem(lane256, 8) == 0, quarter == 0)
    hermit = jnp.where(single, 1.0, 2.0).astype(F32)
    h = jnp.concatenate([x_sums(rh, 0), x_sums(rh, 1)], axis=0) * hermit
    h_high, h_low = halves(h)
    h_both = jnp.concatenate([h_high, h_low], axis=0)

    def spread_one(o, carry):
        picked = jnp.where(lax.div(lane256, 8) == o, h_both, jnp.zeros_like(h_both))
        p = dot(picked, spread[...])
        hx[o] = p[:128] + p[128:]
        return carry

    lax.fori_loop(0, C, spread_one, 0)

    for t in range(2):
        parts = []
        for j in range(2):
            lanes = slice(j * 128, j * 128 + 128)

            def mode_sum(o, carry):
                d_real, d_imag = carry
                h_real = hx[o, t * 64 : t * 64 + 32, lanes]
                h_imag = hx[o, t * 64 + 32 : t * 64 + 64, lanes]
                rows = pl.ds(pl.multiple_of(o * 32, 32), 32)
                w_real = wpack[j, rows, :]
                w_imag = wpack[2 + j, rows, :]
                return (
                    d_real + w_real * h_real + w_imag * h_imag,
                    d_imag + w_real * h_imag - w_imag * h_real,
                )

            zero = jnp.zeros((32, 128), F32)
            d_real, d_imag = lax.fori_loop(0, C, mode_sum, (zero, zero))
            parts.append(jnp.concatenate([d_real, d_imag], axis=0))
        high, low = halves(jnp.concatenate(parts, axis=1))
        x_syn = dot(xs[...], jnp.concatenate([high, low, high], axis=0))
        sr[pl.ds(t * 512, 256, stride=2), :] = x_syn[:, :128]
        sr[pl.ds(t * 512 + 1, 256, stride=2), :] = x_syn[:, 128:]
    own_r = send_all(sr, lambda d: lax.rem(d, 2) * 64 + lax.div(d, 2), rr, me, r_sems, r_sems.at[2])

    arrived(ru, u_sems.at[1])
    own_u.wait()
    u = jnp.concatenate([x_sums(ru, 0), x_sums(ru, 1)], axis=0)
    u_high, u_low = halves(u)
    p = dot(jnp.concatenate([u_high, u_low], axis=0), order[...])
    u = p[:128] + p[128:]

    for j in range(2):
        lanes = slice(j * 128, j * 128 + 128)
        for ah in range(2):
            u_parts = [u[r * 32 + ah * 16 : r * 32 + ah * 16 + 16, lanes] for r in range(4)]

            def outer(o, carry):
                hs = [hx[o, r * 32 + ah * 16 : r * 32 + ah * 16 + 16, lanes] for r in range(4)]
                real = hs[0] * u_parts[0] + hs[1] * u_parts[1] + hs[2] * u_parts[2] + hs[3] * u_parts[3]
                imag = hs[1] * u_parts[0] - hs[0] * u_parts[1] + hs[3] * u_parts[2] - hs[2] * u_parts[3]
                rows = pl.ds(pl.multiple_of(o * 32 + ah * 16, 16), 16)
                gpack[j, rows, :] = real
                gpack[2 + j, rows, :] = imag
                return carry

            lax.fori_loop(0, C, outer, 0)

    def unpack(a, carry):
        for ri in range(2):
            for j in range(2):
                tile = gpack[ri * 2 + j, pl.ds(a, 32, stride=32), :]
                for k in range(4):
                    gout[ri * 32 + a, pl.ds((j * 4 + k) * 32, 32), :] = tile[:, k * 32 : k * 32 + 32]
        return carry

    lax.fori_loop(0, M, unpack, 0)
    copy_grad = pltpu.make_async_copy(gout, grad_hbm, out_sems.at[0])
    copy_grad.start()

    arrived(rr, r_sems.at[1])
    own_r.wait()
    for x in range(2):
        tiles = [[None] * 8 for _ in range(8)]
        for ri in range(2):
            for bo in range(4):
                loaded = [
                    rr[pl.ds(bo * 256 + (n // 2) * 8 + x * 4 + ri * 2 + n % 2, 8, stride=32), :]
                    for n in range(8)
                ]
                for ig, tile in enumerate(exchange_lanes(loaded, 4, lane8)):
                    tiles[ig][ri * 4 + bo] = tile
        for ig in range(8):
            high, low = halves(jnp.concatenate(tiles[ig], axis=0))
            y_syn = dot(ys[...], jnp.concatenate([high, low, high], axis=0))
            high, low = halves(jnp.concatenate([y_syn[:128], y_syn[128:]], axis=1))
            z_syn = dot(high, zh[...]) + dot(low, zh[...]) + dot(high, zl[...])
            for i in range(4):
                total = mixed[ig * 4 + i, x] + z_syn[:, i * 128 : i * 128 + 128]
                fout[ig * 4 + i, x] = total.astype(BF)
    copy_field = pltpu.make_async_copy(fout, field_hbm, out_sems.at[1])
    copy_field.start()
    arrived(sh, h_sems.at[0])
    arrived(su, u_sems.at[0])
    arrived(sr, r_sems.at[0])
    copy_field.wait()
    copy_grad.wait()


def shards(features, pre_act, cotangent, mix_weight, spec_weight):
    planes = (C, 2, G, G)
    consts = tables()
    names = ("wz", "ty", "tx", "xs", "ys", "zh", "zl", "spread", "order", "rep")
    anywhere = pl.BlockSpec(memory_space=pl.ANY)
    inside = pl.BlockSpec(memory_space=pltpu.VMEM)
    message = pltpu.VMEM((NDEV * 8, 128), F32)
    field, grad = pl.pallas_call(
        kernel,
        out_shape=(
            jax.ShapeDtypeStruct(planes, BF),
            jax.ShapeDtypeStruct((64, 256, 32), F32),
        ),
        in_specs=[anywhere] * 3 + [inside] + [anywhere] + [inside] * len(names),
        out_specs=(anywhere, anywhere),
        scratch_shapes=[
            pltpu.VMEM(planes, BF),
            pltpu.VMEM(planes, BF),
            pltpu.VMEM(planes, BF),
            pltpu.VMEM((64, 256, 32), F32),
            pltpu.VMEM(planes, BF),
            pltpu.VMEM((4, 1024, 128), F32),
            pltpu.VMEM((16, 32, 128), F32),
            message, message, message, message, message, message,
            pltpu.VMEM((C, 128, 256), F32),
            pltpu.VMEM((4, 1024, 128), F32),
            pltpu.VMEM((64, 256, 32), F32),
            pltpu.VMEM(planes, F32),
            pltpu.VMEM((512, 512), BF),
            pltpu.VMEM(planes, BF),
            pltpu.SemaphoreType.DMA((4,)),
            pltpu.SemaphoreType.DMA((3,)),
            pltpu.SemaphoreType.DMA((3,)),
            pltpu.SemaphoreType.DMA((3,)),
            pltpu.SemaphoreType.DMA((2,)),
        ],
        compiler_params=pltpu.CompilerParams(
            collective_id=0, has_side_effects=True, vmem_limit_bytes=62 * 2**20
        ),
    )(
        features.reshape(planes),
        pre_act.reshape(planes),
        cotangent.reshape(planes),
        mix_weight,
        spec_weight.reshape(64, 512, 32),
        *[jnp.asarray(consts[name]) for name in names],
    )
    return field.reshape(features.shape), grad.reshape(2, M, 8, C, C)


def solution(mesh):
    placed = P("samp", None, "space", None, None)
    return jax.shard_map(
        shards,
        mesh=mesh,
        in_specs=(placed, placed, placed, P(), P(None, None, "space", None, None)),
        out_specs=(placed, P(None, None, ("space", "samp"), None, None)),
        check_vma=False,
    )
```

profile of v0, /device:TPU:1, one launch (start us, length us, event | category | flops | bytes accessed | tf_op | source)
XLA Modules:
  0.0 70.1 jit_solution(4696445701909808985)
XLA Ops:
  0.6 57.8 %shard_map.158 = (bf16[32,2,128,128]{3,2,1,0:T(8,128)(2,1)}, f32[64,256,32]{2,1,0:T(8,128)}) custom-call(bf16[32,2,128,128]{3,2,1,0:T(8,128)(2,1)} %bitcast.9, bf16[32,2,128,128]{3,2,1,0:T(8,128)(2,1)} %bitcast.10, bf16[32,2,128,128]{3,2,1,0:T(8,128)(2,1)} %bitcast.11, bf16[32,32]{1,0:T(8,128)(2,1)} %mix_ref.1, f32[64,512,32]{2,1,0:T(8,128)} %bitcast.6, ...), custom_call_target="tpu_custom_call" | custom-call | tf_op jit(solution)/shard_map/pallas_call | solution.py:378
  58.4 3.2 %copy.19 = bf16[1,32,2,128,128]{4,3,2,1,0:T(8,128)(2,1)} copy(bf16[1,32,2,128,128]{4,3,2,1,0:T(8,128)(2,1)} %bitcast.8) | data formatting | bytes 4194304
  61.6 8.6 %copy.20 = f32[2,32,8,32,32]{4,3,2,1,0:T(8,128)} copy(f32[2,32,8,32,32]{4,3,2,1,0:T(8,128)} %bitcast.7) | data formatting | bytes 4194304
where the time goes:
time: 70.4 us; the launch traced here: 70.1 us
  Pallas kernels  57.8 us (82%)
  local copies, waits for them, and re-layouts  11.7 us (17%)
    pallas_call x1, Pallas kernels, shards(): pl.pallas_call(kernel, out_shape=(jax.ShapeDtypeStruct(planes, BF), jax.S...  57.8 us
    unnamed x2, local copies, waits for them, and re-layouts  11.7 us

commit v1 on v0

v1 whole, which is shorter than its diff:
```python
import math

import jax
import jax.numpy as jnp
import ml_dtypes
import numpy as np
from jax import lax
from jax.experimental import pallas as pl
from jax.experimental.pallas import tpu as pltpu
from jax.sharding import PartitionSpec as P

MESH = pl.DeviceIdType.MESH
BF = jnp.bfloat16
F32 = jnp.float32
C = 32
M = 32
G = 128
NX = 128
NDEV = 128
NRM = 1.0 / math.sqrt(NX * G * G)


def split_np(values):
    high = values.astype(ml_dtypes.bfloat16)
    low = (values - high.astype(np.float64)).astype(ml_dtypes.bfloat16)
    return high, low


def tables():
    freq = np.arange(M) - M // 2
    pos = np.arange(G)

    def waves(positions, freqs):
        angles = np.mod(positions[:, None] * freqs[None, :], G) * (2.0 * math.pi / G)
        return np.cos(angles), np.sin(angles)

    cos_z, sin_z = waves(pos, np.arange(M))
    cos_c, sin_c = waves(pos, freq)
    cz = cos_z.reshape(G, 4, 8)
    sz = sin_z.reshape(G, 4, 8)
    wz = np.zeros((2, G, 2, 4, 2, 2, 8))
    for x in range(2):
        wz[x, :, 0, :, x, 0] = cz
        wz[x, :, 0, :, x, 1] = -sz
        wz[x, :, 1, :, x, 0] = -sz
        wz[x, :, 1, :, x, 1] = -cz
    wz = wz.reshape(256, 256).astype(ml_dtypes.bfloat16)
    ty = np.concatenate([cos_c.T, sin_c.T], axis=1)
    ty = np.concatenate(split_np(ty), axis=0)
    tx = np.zeros((2, M, NX, 2))
    tx[0, :, :, 0] = cos_c.T
    tx[0, :, :, 1] = sin_c.T
    tx[1, :, :, 0] = -sin_c.T
    tx[1, :, :, 1] = cos_c.T
    tx = tx.reshape(64, 256)
    txh = np.concatenate(split_np(tx * NRM), axis=0)
    xh, xl = split_np(tx.T.copy())
    xs = np.concatenate([xh, xh, xl], axis=1)
    ys = np.zeros((2, G, 2, M))
    ys[0, :, 0] = cos_c
    ys[0, :, 1] = -sin_c
    ys[1, :, 0] = sin_c
    ys[1, :, 1] = cos_c
    yh, yl = split_np(ys.reshape(256, 64) * NRM)
    ys = np.concatenate([yh, yh, yl], axis=1)
    zs = np.zeros((2, 4, 8, 4, 4, G))
    ck = cos_z.T.reshape(8, 4, G).transpose(1, 0, 2)
    sk = sin_z.T.reshape(8, 4, G).transpose(1, 0, 2)
    for i in range(4):
        zs[0, :, :, i, i] = ck
        zs[1, :, :, i, i] = -sk
    zh, zl = split_np(zs.reshape(256, 512))
    eye8 = np.eye(8)
    spread = np.broadcast_to(eye8[None, :, :, None], (C, 8, 8, C)).reshape(256, 256)
    order = np.einsum("cd,kl->ckld", np.eye(C), eye8).reshape(256, 256)
    rep = np.repeat(np.eye(C), 16, axis=0)
    names = dict(wz=wz, ty=ty, tx=txh, xs=xs, ys=ys, zh=zh, zl=zl, spread=spread, order=order, rep=rep)
    return {name: np.ascontiguousarray(v).astype(ml_dtypes.bfloat16) for name, v in names.items()}


def halves(values):
    high = values.astype(BF)
    return high, (values - high.astype(F32)).astype(BF)


def dot(left, right):
    return jnp.dot(left, right, preferred_element_type=F32)


def gelu_slope(values):
    return 0.5 * (1.0 + lax.erf(values * 0.7071067811865476)) + values * (
        jnp.exp(-0.5 * values * values) * 0.3989422804014327
    )


def exchange_lanes(tiles, unit, lane):
    tiles = list(tiles)
    step = 1
    while step < len(tiles):
        keep = (lane // (unit * step)) % 2 == 0
        for i in range(len(tiles)):
            if i & step:
                continue
            low, high = tiles[i], tiles[i | step]
            tiles[i] = jnp.where(keep, low, pltpu.roll(high, unit * step, 1))
            tiles[i | step] = jnp.where(keep, pltpu.roll(low, 128 - unit * step, 1), high)
        step *= 2
    return tiles


def gather(
    feat_hbm, pre_hbm, cot_hbm, mix_ref, spec_hbm,
    wz, ty, tx, xs, spread, order, rep,
    rr, mixed, gout,
    feat, pre, cot, wraw, up, wpack, ysc, sh, su, rh, ru, sr, hx, gpack, kron,
    in_sems, h_sems, u_sems, r_sems,
):
    space = lax.axis_index("space")
    samp = lax.axis_index("samp")
    me = space * 2 + samp
    slot = samp * 64 + space
    quarter = lax.rem(me, 4)

    def parts_of(hbm, vmem, first):
        rows = [pl.ds(part * 8, 8) for part in range(4)]
        return [
            pltpu.make_async_copy(hbm.at[r], vmem.at[r], in_sems.at[first + part])
            for part, r in enumerate(rows)
        ]

    copies_pre = parts_of(pre_hbm, pre, 0)
    copies_cot = parts_of(cot_hbm, cot, 4)
    copies_feat = parts_of(feat_hbm, feat, 8)
    copy_spec = pltpu.make_async_copy(
        spec_hbm.at[:, pl.ds(samp * 256, 256), :], wraw, in_sems.at[12]
    )
    for part in range(4):
        copies_pre[part].start()
        copies_cot[part].start()
    for part in range(4):
        copies_feat[part].start()
    copy_spec.start()

    def device(d):
        return (lax.div(d, 2), lax.rem(d, 2))

    barrier = pltpu.get_barrier_semaphore()

    def greet(j):
        d = lax.rem(me + j, NDEV)
        pl.semaphore_signal(barrier, inc=1, device_id=device(d), device_id_type=MESH)

    lane8 = lax.broadcasted_iota(jnp.int32, (8, 128), 1)

    def spectra(source, half, out, before):
        for cp in range(8):
            c0 = half * 16 + cp * 2
            before(c0)
            z0 = dot(jnp.concatenate([source[c0, 0], source[c0, 1]], axis=1), wz[...])
            z1 = dot(jnp.concatenate([source[c0 + 1, 0], source[c0 + 1, 1]], axis=1), wz[...])
            r = jnp.concatenate(
                [
                    jnp.concatenate([z0[:, :128], z1[:, :128]], axis=1),
                    jnp.concatenate([z0[:, 128:], z1[:, 128:]], axis=1),
                ],
                axis=0,
            )
            high, low = halves(r)
            p = dot(ty[...], high)
            y = p[:32] + p[32:] + dot(ty[0:32, :], low)
            ysc[cp * 2] = y[:, :128]
            ysc[cp * 2 + 1] = y[:, 128:]
        for bo in range(4):
            tiles = [ysc[c, bo * 8 : bo * 8 + 8, :] for c in range(16)]
            tiles = exchange_lanes(tiles, 8, lane8)
            for n in range(16):
                q, xr = n // 4, n % 4
                out[pl.ds(bo * 256 + q * 8 + xr * 2 + half, 8, stride=32), :] = tiles[n]

    def send_all(src, src_at, dst, dst_at, sems, keep_sem):
        def send(j, carry):
            d = lax.rem(me + j, NDEV)
            pltpu.make_async_remote_copy(
                src_ref=src.at[pl.ds(pl.multiple_of(src_at(d) * 8, 8), 8), :],
                dst_ref=dst.at[pl.ds(pl.multiple_of(dst_at * 8, 8), 8), :],
                send_sem=sems.at[0],
                recv_sem=sems.at[1],
                device_id=device(d),
                device_id_type=MESH,
            ).start()
            return carry

        lax.fori_loop(1, NDEV, send, 0)
        own = pltpu.make_async_copy(
            src.at[pl.ds(pl.multiple_of(src_at(me) * 8, 8), 8), :],
            dst.at[pl.ds(pl.multiple_of(dst_at * 8, 8), 8), :],
            keep_sem,
        )
        own.start()
        return own

    def arrived(ref, sem):
        part = ref.at[pl.ds(0, (NDEV - 1) * 8), :]
        pltpu.make_async_copy(part, part, sem).wait()

    def slope(c0):
        if c0 % 8 == 0:
            copies_pre[c0 // 8].wait()
            copies_cot[c0 // 8].wait()
        for c in (c0, c0 + 1):
            for x in range(2):
                values = cot[c, x].astype(F32) * gelu_slope(pre[c, x].astype(F32))
                up[c, x] = values.astype(BF)
        for j in range(c0 * 4, c0 * 4 + 8):
            if j:
                greet(j)

    for half in range(2):
        spectra(up, half, sh, slope)
    pl.semaphore_wait(barrier, NDEV - 1)
    own_h = send_all(sh, lambda d: d, rh, slot, h_sems, h_sems.at[2])

    def loaded_feat(c0):
        if c0 % 8 == 0:
            copies_feat[c0 // 8].wait()

    for half in range(2):
        spectra(feat, half, su, loaded_feat)
    own_u = send_all(su, lambda d: d, ru, slot, u_sems, u_sems.at[2])

    copy_spec.wait()

    def pack(a, carry):
        for ri in range(2):
            for j in range(2):
                parts = [
                    wraw[ri * 32 + a, pl.ds((j * 4 + k) * 32, 32), :] for k in range(4)
                ]
                wpack[ri * 2 + j, pl.ds(a, 32, stride=32), :] = jnp.concatenate(parts, axis=1)
        return carry

    lax.fori_loop(0, M, pack, 0)

    def x_sums(ref, t):
        r = jnp.concatenate(
            [ref[pl.ds(t * 512, 256, stride=2), :], ref[pl.ds(t * 512 + 1, 256, stride=2), :]],
            axis=1,
        )
        high, low = halves(r)
        p = dot(tx[...], high)
        return p[:64] + p[64:] + dot(tx[0:64, :], low)

    arrived(rh, h_sems.at[1])
    own_h.wait()
    lane256 = lax.broadcasted_iota(jnp.int32, (1, 256), 1)
    single = jnp.logical_and(lax.rem(lane256, 8) == 0, quarter == 0)
    hermit = jnp.where(single, 1.0, 2.0).astype(F32)
    h = jnp.concatenate([x_sums(rh, 0), x_sums(rh, 1)], axis=0) * hermit
    h_high, h_low = halves(h)
    h_both = jnp.concatenate([h_high, h_low], axis=0)

    def mode_sum(o, sums):
        picked = jnp.where(lax.div(lane256, 8) == o, h_both, jnp.zeros_like(h_both))
        p = dot(picked, spread[...])
        spread_h = p[:128] + p[128:]
        hx[o] = spread_h
        rows = pl.ds(pl.multiple_of(o * 32, 32), 32)
        later = []
        for j in range(2):
            w_real = wpack[j, rows, :]
            w_imag = wpack[2 + j, rows, :]
            for t in range(2):
                h_real = spread_h[t * 64 : t * 64 + 32, j * 128 : j * 128 + 128]
                h_imag = spread_h[t * 64 + 32 : t * 64 + 64, j * 128 : j * 128 + 128]
                d_real, d_imag = sums[(j * 2 + t) * 2], sums[(j * 2 + t) * 2 + 1]
                later.append(d_real + w_real * h_real + w_imag * h_imag)
                later.append(d_imag + w_real * h_imag - w_imag * h_real)
        return tuple(later)

    zero = jnp.zeros((32, 128), F32)
    sums = lax.fori_loop(0, C, mode_sum, (zero,) * 8, unroll=4)
    for t in range(2):
        left = jnp.concatenate([sums[t * 2], sums[t * 2 + 1]], axis=0)
        right = jnp.concatenate([sums[4 + t * 2], sums[5 + t * 2]], axis=0)
        high, low = halves(jnp.concatenate([left, right], axis=1))
        x_syn = dot(xs[...], jnp.concatenate([high, low, high], axis=0))
        sr[pl.ds(t * 512, 256, stride=2), :] = x_syn[:, :128]
        sr[pl.ds(t * 512 + 1, 256, stride=2), :] = x_syn[:, 128:]
    own_r = send_all(sr, lambda d: lax.rem(d, 2) * 64 + lax.div(d, 2), rr, me, r_sems, r_sems.at[2])

    arrived(ru, u_sems.at[1])
    own_u.wait()
    u = jnp.concatenate([x_sums(ru, 0), x_sums(ru, 1)], axis=0)
    u_high, u_low = halves(u)
    p = dot(jnp.concatenate([u_high, u_low], axis=0), order[...])
    u = p[:128] + p[128:]

    for j in range(2):
        lanes = slice(j * 128, j * 128 + 128)
        for ah in range(2):
            u_parts = [u[r * 32 + ah * 16 : r * 32 + ah * 16 + 16, lanes] for r in range(4)]

            def outer(o, carry):
                hs = [hx[o, r * 32 + ah * 16 : r * 32 + ah * 16 + 16, lanes] for r in range(4)]
                real = hs[0] * u_parts[0] + hs[1] * u_parts[1] + hs[2] * u_parts[2] + hs[3] * u_parts[3]
                imag = hs[1] * u_parts[0] - hs[0] * u_parts[1] + hs[3] * u_parts[2] - hs[2] * u_parts[3]
                rows = pl.ds(pl.multiple_of(o * 32 + ah * 16, 16), 16)
                gpack[j, rows, :] = real
                gpack[2 + j, rows, :] = imag
                return carry

            lax.fori_loop(0, C, outer, 0)

    def unpack(a, carry):
        for ri in range(2):
            for j in range(2):
                tile = gpack[ri * 2 + j, pl.ds(a, 32, stride=32), :]
                for k in range(4):
                    gout[ri * 32 + a, pl.ds((j * 4 + k) * 32, 32), :] = tile[:, k * 32 : k * 32 + 32]
        return carry

    lax.fori_loop(0, M, unpack, 0)

    turned = lax.dot_general(
        rep[...], mix_ref[...], (((1,), (1,)), ((), ())), preferred_element_type=F32
    ).astype(BF)
    wide = lax.dot_general(
        turned, rep[...], (((1,), (1,)), ((), ())), preferred_element_type=F32
    )
    row = lax.broadcasted_iota(jnp.int32, (512, 512), 0)
    col = lax.broadcasted_iota(jnp.int32, (512, 512), 1)
    kron[...] = jnp.where(lax.rem(row, 16) == lax.rem(col, 16), wide, 0.0).astype(BF)

    def mixing(yb, carry):
        y0 = pl.multiple_of(yb * 16, 16)
        for x in range(2):
            block = up[:, x, pl.ds(y0, 16), :].reshape(512, 128)
            mixed[:, x, pl.ds(y0, 16), :] = dot(kron[...], block).reshape(C, 16, 128)
        return carry

    lax.fori_loop(0, 8, mixing, 0)

    arrived(rr, r_sems.at[1])
    own_r.wait()
    arrived(sh, h_sems.at[0])
    arrived(su, u_sems.at[0])
    arrived(sr, r_sems.at[0])


def synthesis(rr, mixed, gout, ys, zh, zl, field_hbm, grad_hbm, fout, sems):
    lane8 = lax.broadcasted_iota(jnp.int32, (8, 128), 1)
    copy_grad = pltpu.make_async_copy(gout, grad_hbm, sems.at[8])
    copy_grad.start()
    tiles = [[[None] * 8 for _ in range(8)] for _ in range(2)]
    for x in range(2):
        for ri in range(2):
            for bo in range(4):
                loaded = [
                    rr[pl.ds(bo * 256 + (n // 2) * 8 + x * 4 + ri * 2 + n % 2, 8, stride=32), :]
                    for n in range(8)
                ]
                for ig, tile in enumerate(exchange_lanes(loaded, 4, lane8)):
                    tiles[x][ig][ri * 4 + bo] = tile
    copies = []
    for ig in range(8):
        for x in range(2):
            high, low = halves(jnp.concatenate(tiles[x][ig], axis=0))
            y_syn = dot(ys[...], jnp.concatenate([high, low, high], axis=0))
            high, low = halves(jnp.concatenate([y_syn[:128], y_syn[128:]], axis=1))
            z_syn = dot(high, zh[...]) + dot(low, zh[...]) + dot(high, zl[...])
            for i in range(4):
                total = mixed[ig * 4 + i, x] + z_syn[:, i * 128 : i * 128 + 128]
                fout[ig * 4 + i, x] = total.astype(BF)
        rows = pl.ds(ig * 4, 4)
        copies.append(pltpu.make_async_copy(fout.at[rows], field_hbm.at[rows], sems.at[ig]))
        copies[-1].start()
    for copy in copies:
        copy.wait()
    copy_grad.wait()


def shards(features, pre_act, cotangent, mix_weight, spec_weight):
    planes = (C, 2, G, G)
    consts = tables()
    anywhere = pl.BlockSpec(memory_space=pl.ANY)
    inside = pl.BlockSpec(memory_space=pltpu.VMEM)
    message = pltpu.VMEM((NDEV * 8, 128), F32)
    grad_shape = (64, 256, 32)
    first = ("wz", "ty", "tx", "xs", "spread", "order", "rep")
    returned, mixed, grad = pl.pallas_call(
        gather,
        out_shape=(
            pltpu.VMEM((NDEV * 8, 128), F32),
            pltpu.VMEM(planes, F32),
            pltpu.VMEM(grad_shape, F32),
        ),
        in_specs=[anywhere] * 3 + [inside] + [anywhere] + [inside] * len(first),
        out_specs=(inside, inside, inside),
        scratch_shapes=[
            pltpu.VMEM(planes, BF),
            pltpu.VMEM(planes, BF),
            pltpu.VMEM(planes, BF),
            pltpu.VMEM(grad_shape, F32),
            pltpu.VMEM(planes, BF),
            pltpu.VMEM((4, 1024, 128), F32),
            pltpu.VMEM((16, 32, 128), F32),
            message, message, message, message, message,
            pltpu.VMEM((C, 128, 256), F32),
            pltpu.VMEM((4, 1024, 128), F32),
            pltpu.VMEM((512, 512), BF),
            pltpu.SemaphoreType.DMA((13,)),
            pltpu.SemaphoreType.DMA((3,)),
            pltpu.SemaphoreType.DMA((3,)),
            pltpu.SemaphoreType.DMA((3,)),
        ],
        compiler_params=pltpu.CompilerParams(
            collective_id=0, has_side_effects=True, vmem_limit_bytes=44 * 2**20
        ),
    )(
        features.reshape(planes),
        pre_act.reshape(planes),
        cotangent.reshape(planes),
        mix_weight,
        spec_weight.reshape(64, 512, 32),
        *[jnp.asarray(consts[name]) for name in first],
    )
    second = ("ys", "zh", "zl")
    field, grad = pl.pallas_call(
        synthesis,
        out_shape=(
            jax.ShapeDtypeStruct(planes, BF),
            jax.ShapeDtypeStruct(grad_shape, F32),
        ),
        in_specs=[inside] * (3 + len(second)),
        out_specs=(anywhere, anywhere),
        scratch_shapes=[
            pltpu.VMEM(planes, BF),
            pltpu.SemaphoreType.DMA((9,)),
        ],
        compiler_params=pltpu.CompilerParams(vmem_limit_bytes=40 * 2**20),
    )(returned, mixed, grad, *[jnp.asarray(consts[name]) for name in second])
    return field.reshape(features.shape), grad.reshape(2, M, 8, C, C)


def solution(mesh):
    placed = P("samp", None, "space", None, None)
    return jax.shard_map(
        shards,
        mesh=mesh,
        in_specs=(placed, placed, placed, P(), P(None, None, "space", None, None)),
        out_specs=(placed, P(None, None, ("space", "samp"), None, None)),
        check_vma=False,
    )
```

time: 70.4 us -> 51.8 us (0.74)
  the two profiles are of different devices: /device:TPU:1 before, /device:TPU:3 now
where the time goes in v1:
time: 51.8 us; the launch traced here: 51.7 us
  Pallas kernels  50.8 us (98%)
  between operations  0.85 us (2%)
    pallas_call x1, Pallas kernels, shards(): pl.pallas_call(gather, out_shape=(pltpu.VMEM((NDEV * 8, 128), F32), pltpu...  46.4 us
    pallas_call x1, Pallas kernels, shards(): pl.pallas_call(synthesis, out_shape=(jax.ShapeDtypeStruct(planes, BF), ja...  4.42 us

profile of v1, /device:TPU:3, one launch (start us, length us, event | category | flops | bytes accessed | tf_op | source)
XLA Modules:
  0.0 51.7 jit_solution(3185636983516544397)
XLA Ops:
  0.6 0.0 copy-start
  0.6 0.0 copy-start.1
  0.7 0.0 copy-start.2
  0.7 46.4 %shard_map.158 = (f32[1024,128]{1,0:T(8,128)S(1)}, f32[32,2,128,128]{3,2,1,0:T(8,128)S(1)}, f32[64,256,32]{2,1,0:T(8,128)S(1)}) custom-call(bf16[32,2,128,128]{3,2,1,0:T(8,128)(2,1)} %bitcast.7, bf16[32,2,128,128]{3,2,1,0:T(8,128)(2,1)} %bitcast.8, bf16[32,2,128,128]{3,2,1,0:T(8,128)(2,1)} %bitcast.9, bf16[32,32]{1,0:T(8,128)(2,1)} %mix_ref.1, ...), custom_call_target="tpu_custom_call" | custom-call | tf_op jit(solution)/shard_map/pallas_call | solution.py:390
  47.1 0.0 copy-done
  47.1 0.0 copy-done.1
  47.1 0.0 copy-done.2
  47.1 4.4 %shard_map.159 = (bf16[32,2,128,128]{3,2,1,0:T(8,128)(2,1)}, f32[64,256,32]{2,1,0:T(8,128)}) custom-call(f32[1024,128]{1,0:T(8,128)S(1)} %get-tuple-element.7.rr, f32[32,2,128,128]{3,2,1,0:T(8,128)S(1)} %get-tuple-element.8.mixed, f32[64,256,32]{2,1,0:T(8,128)S(1)} %get-tuple-element.9.gout, bf16[256,192]{1,0:T(8,128)(2,1)S(1)} %copy-done.2, ...), custom_call_target="tpu_custom_call" | custom-call | tf_op jit(solution)/shard_map/pallas_call | solution.py:428
Async XLA Ops:
  0.6 46.4 %copy-start = (bf16[256,512]{1,0:T(8,128)(2,1)S(1)}, bf16[256,512]{1,0:T(8,128)(2,1)}, u32[]{:S(2)}) copy-start(bf16[256,512]{1,0:T(8,128)(2,1)} %constant.29.clone.zl) | copy-start | bytes 786436
  0.6 46.4 %copy-start.1 = (bf16[256,512]{1,0:T(8,128)(2,1)S(1)}, bf16[256,512]{1,0:T(8,128)(2,1)}, u32[]{:S(2)}) copy-start(bf16[256,512]{1,0:T(8,128)(2,1)} %constant.28.clone.zh) | copy-start | bytes 786436
  0.7 46.4 %copy-start.2 = (bf16[256,192]{1,0:T(8,128)(2,1)S(1)}, bf16[256,192]{1,0:T(8,128)(2,1)}, u32[]{:S(2)}) copy-start(bf16[256,192]{1,0:T(8,128)(2,1)} %constant.27.clone.ys) | copy-start | bytes 294916

commit v2 on v1

--- a/solution.py
+++ b/solution.py
@@ -113,7 +113,7 @@
     wz, ty, tx, xs, spread, order, rep,
     rr, mixed, gout,
     feat, pre, cot, wraw, up, wpack, ysc, sh, su, rh, ru, sr, hx, gpack, kron,
-    in_sems, h_sems, u_sems, r_sems,
+    in_sems, h_sems, u_sems, r_sems, relay,
 ):
     space = lax.axis_index("space")
     samp = lax.axis_index("samp")
@@ -135,10 +135,9 @@
         spec_hbm.at[:, pl.ds(samp * 256, 256), :], wraw, in_sems.at[12]
     )
     for part in range(4):
+        copies_feat[part].start()
         copies_pre[part].start()
         copies_cot[part].start()
-    for part in range(4):
-        copies_feat[part].start()
     copy_spec.start()
 
     def device(d):
@@ -146,58 +145,70 @@
 
     barrier = pltpu.get_barrier_semaphore()
 
-    def greet(j):
-        d = lax.rem(me + j, NDEV)
-        pl.semaphore_signal(barrier, inc=1, device_id=device(d), device_id_type=MESH)
+    def signal(sem, j):
+        d = jnp.bitwise_and(me + j, NDEV - 1)
+        pl.semaphore_signal(sem, inc=1, device_id=device(d), device_id_type=MESH)
+
+    for j in range(1, 8):
+        signal(barrier, NDEV - j)
+    for j in range(8, NDEV, 8):
+        signal(barrier, j)
+
+    def relay_entry():
+        pl.semaphore_wait(barrier, 22)
+        for j in range(1, 8):
+            signal(relay, j)
 
     lane8 = lax.broadcasted_iota(jnp.int32, (8, 128), 1)
 
-    def spectra(source, half, out, before):
-        for cp in range(8):
-            c0 = half * 16 + cp * 2
-            before(c0)
-            z0 = dot(jnp.concatenate([source[c0, 0], source[c0, 1]], axis=1), wz[...])
-            z1 = dot(jnp.concatenate([source[c0 + 1, 0], source[c0 + 1, 1]], axis=1), wz[...])
-            r = jnp.concatenate(
-                [
-                    jnp.concatenate([z0[:, :128], z1[:, :128]], axis=1),
-                    jnp.concatenate([z0[:, 128:], z1[:, 128:]], axis=1),
-                ],
-                axis=0,
-            )
-            high, low = halves(r)
-            p = dot(ty[...], high)
-            y = p[:32] + p[32:] + dot(ty[0:32, :], low)
-            ysc[cp * 2] = y[:, :128]
-            ysc[cp * 2 + 1] = y[:, 128:]
+    def sums_of(source, c0):
+        z0 = dot(jnp.concatenate([source[c0, 0], source[c0, 1]], axis=1), wz[...])
+        z1 = dot(jnp.concatenate([source[c0 + 1, 0], source[c0 + 1, 1]], axis=1), wz[...])
+        r = jnp.concatenate(
+            [
+                jnp.concatenate([z0[:, :128], z1[:, :128]], axis=1),
+                jnp.concatenate([z0[:, 128:], z1[:, 128:]], axis=1),
+            ],
+            axis=0,
+        )
+        high, low = halves(r)
+        p = dot(ty[...], high)
+        y = p[:32] + p[32:] + dot(ty[0:32, :], low)
+        ysc[c0] = y[:, :128]
+        ysc[c0 + 1] = y[:, 128:]
+
+    def to_messages(half, out):
         for bo in range(4):
-            tiles = [ysc[c, bo * 8 : bo * 8 + 8, :] for c in range(16)]
+            tiles = [ysc[half * 16 + c, bo * 8 : bo * 8 + 8, :] for c in range(16)]
             tiles = exchange_lanes(tiles, 8, lane8)
             for n in range(16):
                 q, xr = n // 4, n % 4
                 out[pl.ds(bo * 256 + q * 8 + xr * 2 + half, 8, stride=32), :] = tiles[n]
 
-    def send_all(src, src_at, dst, dst_at, sems, keep_sem):
-        def send(j, carry):
-            d = lax.rem(me + j, NDEV)
+    def sender(src, src_at, dst, dst_at, sems):
+        to_rows = pl.ds(pl.multiple_of(dst_at * 8, 8), 8)
+
+        def send(j):
+            d = jnp.bitwise_and(me + j, NDEV - 1)
             pltpu.make_async_remote_copy(
                 src_ref=src.at[pl.ds(pl.multiple_of(src_at(d) * 8, 8), 8), :],
-                dst_ref=dst.at[pl.ds(pl.multiple_of(dst_at * 8, 8), 8), :],
+                dst_ref=dst.at[to_rows, :],
                 send_sem=sems.at[0],
                 recv_sem=sems.at[1],
                 device_id=device(d),
                 device_id_type=MESH,
             ).start()
-            return carry
-
-        lax.fori_loop(1, NDEV, send, 0)
+
         own = pltpu.make_async_copy(
-            src.at[pl.ds(pl.multiple_of(src_at(me) * 8, 8), 8), :],
-            dst.at[pl.ds(pl.multiple_of(dst_at * 8, 8), 8), :],
-            keep_sem,
+            src.at[pl.ds(pl.multiple_of(src_at(me) * 8, 8), 8), :], dst.at[to_rows, :], sems.at[2]
         )
-        own.start()
-        return own
+        return send, own
+
+    send_h, own_h = sender(sh, lambda d: d, rh, slot, h_sems)
+    send_u, own_u = sender(su, lambda d: d, ru, slot, u_sems)
+    send_r, own_r = sender(
+        sr, lambda d: lax.rem(d, 2) * 64 + lax.div(d, 2), rr, me, r_sems
+    )
 
     def arrived(ref, sem):
         part = ref.at[pl.ds(0, (NDEV - 1) * 8), :]
@@ -211,22 +222,29 @@
             for x in range(2):
                 values = cot[c, x].astype(F32) * gelu_slope(pre[c, x].astype(F32))
                 up[c, x] = values.astype(BF)
-        for j in range(c0 * 4, c0 * 4 + 8):
-            if j:
-                greet(j)
-
-    for half in range(2):
-        spectra(up, half, sh, slope)
-    pl.semaphore_wait(barrier, NDEV - 1)
-    own_h = send_all(sh, lambda d: d, rh, slot, h_sems, h_sems.at[2])
-
-    def loaded_feat(c0):
-        if c0 % 8 == 0:
-            copies_feat[c0 // 8].wait()
-
-    for half in range(2):
-        spectra(feat, half, su, loaded_feat)
-    own_u = send_all(su, lambda d: d, ru, slot, u_sems, u_sems.at[2])
+
+    for step in range(8):
+        for c0 in (step * 4, step * 4 + 2):
+            if c0 % 8 == 0:
+                copies_feat[c0 // 8].wait()
+            sums_of(feat, c0)
+        if step == 1:
+            relay_entry()
+        if step % 4 == 3:
+            to_messages(step // 4, su)
+
+    pl.semaphore_wait(relay, 7)
+    own_u.start()
+    for j in range(1, NDEV):
+        send_u(j)
+    for step in range(16):
+        slope(step * 2)
+        sums_of(up, step * 2)
+        if step % 8 == 7:
+            to_messages(step // 8, sh)
+    own_h.start()
+    for j in range(1, NDEV):
+        send_h(j)
 
     copy_spec.wait()
 
@@ -241,6 +259,16 @@
 
     lax.fori_loop(0, M, pack, 0)
 
+    turned = lax.dot_general(
+        rep[...], mix_ref[...], (((1,), (1,)), ((), ())), preferred_element_type=F32
+    ).astype(BF)
+    wide = lax.dot_general(
+        turned, rep[...], (((1,), (1,)), ((), ())), preferred_element_type=F32
+    )
+    row = lax.broadcasted_iota(jnp.int32, (512, 512), 0)
+    col = lax.broadcasted_iota(jnp.int32, (512, 512), 1)
+    kron[...] = jnp.where(lax.rem(row, 16) == lax.rem(col, 16), wide, 0.0).astype(BF)
+
     def x_sums(ref, t):
         r = jnp.concatenate(
             [ref[pl.ds(t * 512, 256, stride=2), :], ref[pl.ds(t * 512 + 1, 256, stride=2), :]],
@@ -249,6 +277,13 @@
         high, low = halves(r)
         p = dot(tx[...], high)
         return p[:64] + p[64:] + dot(tx[0:64, :], low)
+
+    arrived(ru, u_sems.at[1])
+    own_u.wait()
+    u = jnp.concatenate([x_sums(ru, 0), x_sums(ru, 1)], axis=0)
+    u_high, u_low = halves(u)
+    p = dot(jnp.concatenate([u_high, u_low], axis=0), order[...])
+    u = p[:128] + p[128:]
 
     arrived(rh, h_sems.at[1])
     own_h.wait()
@@ -286,14 +321,18 @@
         x_syn = dot(xs[...], jnp.concatenate([high, low, high], axis=0))
         sr[pl.ds(t * 512, 256, stride=2), :] = x_syn[:, :128]
         sr[pl.ds(t * 512 + 1, 256, stride=2), :] = x_syn[:, 128:]
-    own_r = send_all(sr, lambda d: lax.rem(d, 2) * 64 + lax.div(d, 2), rr, me, r_sems, r_sems.at[2])
-
-    arrived(ru, u_sems.at[1])
-    own_u.wait()
-    u = jnp.concatenate([x_sums(ru, 0), x_sums(ru, 1)], axis=0)
-    u_high, u_low = halves(u)
-    p = dot(jnp.concatenate([u_high, u_low], axis=0), order[...])
-    u = p[:128] + p[128:]
+    own_r.start()
+    def mixing(yb):
+        y0 = yb * 16
+        for x in range(2):
+            block = up[:, x, y0 : y0 + 16, :].reshape(512, 128)
+            mixed[:, x, y0 : y0 + 16, :] = dot(kron[...], block).reshape(C, 16, 128)
+
+    for j in range(1, NDEV):
+        send_r(j)
+    for yb in range(8):
+        mixing(yb)
+
 
     for j in range(2):
         lanes = slice(j * 128, j * 128 + 128)
@@ -320,25 +359,6 @@
         return carry
 
     lax.fori_loop(0, M, unpack, 0)
-
-    turned = lax.dot_general(
-        rep[...], mix_ref[...], (((1,), (1,)), ((), ())), preferred_element_type=F32
-    ).astype(BF)
-    wide = lax.dot_general(
-        turned, rep[...], (((1,), (1,)), ((), ())), preferred_element_type=F32
-    )
-    row = lax.broadcasted_iota(jnp.int32, (512, 512), 0)
-    col = lax.broadcasted_iota(jnp.int32, (512, 512), 1)
-    kron[...] = jnp.where(lax.rem(row, 16) == lax.rem(col, 16), wide, 0.0).astype(BF)
-
-    def mixing(yb, carry):
-        y0 = pl.multiple_of(yb * 16, 16)
-        for x in range(2):
-            block = up[:, x, pl.ds(y0, 16), :].reshape(512, 128)
-            mixed[:, x, pl.ds(y0, 16), :] = dot(kron[...], block).reshape(C, 16, 128)
-        return carry
-
-    lax.fori_loop(0, 8, mixing, 0)
 
     arrived(rr, r_sems.at[1])
     own_r.wait()
@@ -403,7 +423,7 @@
             pltpu.VMEM(grad_shape, F32),
             pltpu.VMEM(planes, BF),
             pltpu.VMEM((4, 1024, 128), F32),
-            pltpu.VMEM((16, 32, 128), F32),
+            pltpu.VMEM((C, 32, 128), F32),
             message, message, message, message, message,
             pltpu.VMEM((C, 128, 256), F32),
             pltpu.VMEM((4, 1024, 128), F32),
@@ -412,6 +432,7 @@
             pltpu.SemaphoreType.DMA((3,)),
             pltpu.SemaphoreType.DMA((3,)),
             pltpu.SemaphoreType.DMA((3,)),
+            pltpu.SemaphoreType.REGULAR,
         ],
         compiler_params=pltpu.CompilerParams(
             collective_id=0, has_side_effects=True, vmem_limit_bytes=44 * 2**20

time: 51.8 us -> 46.4 us (0.90)
  the two profiles are of different devices: /device:TPU:3 before, /device:TPU:1 now
where the time goes in v2:
time: 46.4 us; the launch traced here: 46.2 us
  Pallas kernels  45.4 us (98%)
  between operations  0.85 us (2%)
    pallas_call x1, Pallas kernels, shards(): pl.pallas_call(gather, out_shape=(pltpu.VMEM((NDEV * 8, 128), F32), pltpu...  41 us
    pallas_call x1, Pallas kernels, shards(): pl.pallas_call(synthesis, out_shape=(jax.ShapeDtypeStruct(planes, BF), ja...  4.42 us

profile of v2, /device:TPU:1, one launch (start us, length us, event | category | flops | bytes accessed | tf_op | source)
XLA Modules:
  0.0 46.2 jit_solution(10362614782910832662)
XLA Ops:
  0.6 0.0 copy-start
  0.6 0.0 copy-start.1
  0.7 0.0 copy-start.2
  0.7 41.0 %shard_map.158 = (f32[1024,128]{1,0:T(8,128)S(1)}, f32[32,2,128,128]{3,2,1,0:T(8,128)S(1)}, f32[64,256,32]{2,1,0:T(8,128)S(1)}) custom-call(bf16[32,2,128,128]{3,2,1,0:T(8,128)(2,1)} %bitcast.7, bf16[32,2,128,128]{3,2,1,0:T(8,128)(2,1)} %bitcast.8, bf16[32,2,128,128]{3,2,1,0:T(8,128)(2,1)} %bitcast.9, bf16[32,32]{1,0:T(8,128)(2,1)} %mix_ref.1, ...), custom_call_target="tpu_custom_call" | custom-call | tf_op jit(solution)/shard_map/pallas_call | solution.py:410
  41.6 0.0 copy-done
  41.6 0.0 copy-done.1
  41.7 0.0 copy-done.2
  41.7 4.4 %shard_map.159 = (bf16[32,2,128,128]{3,2,1,0:T(8,128)(2,1)}, f32[64,256,32]{2,1,0:T(8,128)}) custom-call(f32[1024,128]{1,0:T(8,128)S(1)} %get-tuple-element.7.rr, f32[32,2,128,128]{3,2,1,0:T(8,128)S(1)} %get-tuple-element.8.mixed, f32[64,256,32]{2,1,0:T(8,128)S(1)} %get-tuple-element.9.gout, bf16[256,192]{1,0:T(8,128)(2,1)S(1)} %copy-done.2, ...), custom_call_target="tpu_custom_call" | custom-call | tf_op jit(solution)/shard_map/pallas_call | solution.py:449
Async XLA Ops:
  0.6 41.0 %copy-start = (bf16[256,512]{1,0:T(8,128)(2,1)S(1)}, bf16[256,512]{1,0:T(8,128)(2,1)}, u32[]{:S(2)}) copy-start(bf16[256,512]{1,0:T(8,128)(2,1)} %constant.29.clone.zl) | copy-start | bytes 786436
  0.6 41.0 %copy-start.1 = (bf16[256,512]{1,0:T(8,128)(2,1)S(1)}, bf16[256,512]{1,0:T(8,128)(2,1)}, u32[]{:S(2)}) copy-start(bf16[256,512]{1,0:T(8,128)(2,1)} %constant.28.clone.zh) | copy-start | bytes 786436
  0.7 41.0 %copy-start.2 = (bf16[256,192]{1,0:T(8,128)(2,1)S(1)}, bf16[256,192]{1,0:T(8,128)(2,1)}, u32[]{:S(2)}) copy-start(bf16[256,192]{1,0:T(8,128)(2,1)} %constant.27.clone.ys) | copy-start | bytes 294916

commit v3 on v2

--- a/solution.py
+++ b/solution.py
@@ -109,11 +109,12 @@
 
 
 def gather(
-    feat_hbm, pre_hbm, cot_hbm, mix_ref, spec_hbm,
-    wz, ty, tx, xs, spread, order, rep,
+    feat_hbm, pre_hbm, cot_hbm, mix_hbm, spec_hbm,
+    wz_hbm, ty_hbm, tx_hbm, xs_hbm, spread_hbm, order_hbm, rep_hbm,
     rr, mixed, gout,
     feat, pre, cot, wraw, up, wpack, ysc, sh, su, rh, ru, sr, hx, gpack, kron,
-    in_sems, h_sems, u_sems, r_sems, relay,
+    mix_ref, wz, ty, tx, xs, spread, order, rep,
+    in_sems, table_sems, h_sems, u_sems, r_sems, relay,
 ):
     space = lax.axis_index("space")
     samp = lax.axis_index("samp")
@@ -134,10 +135,24 @@
     copy_spec = pltpu.make_async_copy(
         spec_hbm.at[:, pl.ds(samp * 256, 256), :], wraw, in_sems.at[12]
     )
+    table_pairs = (
+        (wz_hbm, wz), (ty_hbm, ty), (mix_hbm, mix_ref), (tx_hbm, tx),
+        (xs_hbm, xs), (spread_hbm, spread), (order_hbm, order), (rep_hbm, rep),
+    )
+    copies_table = [
+        pltpu.make_async_copy(hbm, vmem, table_sems.at[i])
+        for i, (hbm, vmem) in enumerate(table_pairs)
+    ]
+    copies_feat[0].start()
+    copies_table[0].start()
+    copies_table[1].start()
     for part in range(4):
-        copies_feat[part].start()
+        if part:
+            copies_feat[part].start()
         copies_pre[part].start()
         copies_cot[part].start()
+    for copy in copies_table[2:]:
+        copy.start()
     copy_spec.start()
 
     def device(d):
@@ -223,6 +238,8 @@
                 values = cot[c, x].astype(F32) * gelu_slope(pre[c, x].astype(F32))
                 up[c, x] = values.astype(BF)
 
+    copies_table[0].wait()
+    copies_table[1].wait()
     for step in range(8):
         for c0 in (step * 4, step * 4 + 2):
             if c0 % 8 == 0:
@@ -246,6 +263,8 @@
     for j in range(1, NDEV):
         send_h(j)
 
+    for copy in copies_table[2:]:
+        copy.wait()
     copy_spec.wait()
 
     def pack(a, carry):
@@ -292,12 +311,11 @@
     hermit = jnp.where(single, 1.0, 2.0).astype(F32)
     h = jnp.concatenate([x_sums(rh, 0), x_sums(rh, 1)], axis=0) * hermit
     h_high, h_low = halves(h)
-    h_both = jnp.concatenate([h_high, h_low], axis=0)
+    h_both = h_high
 
     def mode_sum(o, sums):
         picked = jnp.where(lax.div(lane256, 8) == o, h_both, jnp.zeros_like(h_both))
-        p = dot(picked, spread[...])
-        spread_h = p[:128] + p[128:]
+        spread_h = dot(picked, spread[...])
         hx[o] = spread_h
         rows = pl.ds(pl.multiple_of(o * 32, 32), 32)
         later = []
@@ -414,7 +432,7 @@
             pltpu.VMEM(planes, F32),
             pltpu.VMEM(grad_shape, F32),
         ),
-        in_specs=[anywhere] * 3 + [inside] + [anywhere] + [inside] * len(first),
+        in_specs=[anywhere] * (5 + len(first)),
         out_specs=(inside, inside, inside),
         scratch_shapes=[
             pltpu.VMEM(planes, BF),
@@ -428,7 +446,10 @@
             pltpu.VMEM((C, 128, 256), F32),
             pltpu.VMEM((4, 1024, 128), F32),
             pltpu.VMEM((512, 512), BF),
+            pltpu.VMEM((C, C), BF),
+            *[pltpu.VMEM(consts[name].shape, BF) for name in first],
             pltpu.SemaphoreType.DMA((13,)),
+            pltpu.SemaphoreType.DMA((8,)),
             pltpu.SemaphoreType.DMA((3,)),
             pltpu.SemaphoreType.DMA((3,)),
             pltpu.SemaphoreType.DMA((3,)),

time: 46.4 us -> 44.7 us (0.963)
  Pallas kernels: 45.4 us -> 43.7 us
    pallas_call x1, Pallas kernels: 41 us -> 39.3 us  [shards(): pl.pallas_call(gather, out_shape=(pltpu.VMEM((NDEV * 8, 128), F32), pltpu...]
where the time goes in v3:
time: 44.7 us; the launch traced here: 44.6 us
  Pallas kernels  43.7 us (98%)
  between operations  0.85 us (2%)
    pallas_call x1, Pallas kernels, shards(): pl.pallas_call(gather, out_shape=(pltpu.VMEM((NDEV * 8, 128), F32), pltpu...  39.3 us
    pallas_call x1, Pallas kernels, shards(): pl.pallas_call(synthesis, out_shape=(jax.ShapeDtypeStruct(planes, BF), ja...  4.42 us

profile of v3, /device:TPU:1, one launch (start us, length us, event | category | flops | bytes accessed | tf_op | source)
XLA Modules:
  0.0 44.6 jit_solution(5638892905404773777)
XLA Ops:
  0.6 0.0 copy-start
  0.6 0.0 copy-start.1
  0.7 0.0 copy-start.2
  0.7 39.3 %shard_map.158 = (f32[1024,128]{1,0:T(8,128)S(1)}, f32[32,2,128,128]{3,2,1,0:T(8,128)S(1)}, f32[64,256,32]{2,1,0:T(8,128)S(1)}) custom-call(bf16[32,2,128,128]{3,2,1,0:T(8,128)(2,1)} %bitcast.7, bf16[32,2,128,128]{3,2,1,0:T(8,128)(2,1)} %bitcast.8, bf16[32,2,128,128]{3,2,1,0:T(8,128)(2,1)} %bitcast.9, bf16[32,32]{1,0:T(8,128)(2,1)} %mix_hbm.1, ...), custom_call_target="tpu_custom_call" | custom-call | tf_op jit(solution)/shard_map/pallas_call | solution.py:428
  40.0 0.0 copy-done
  40.0 0.0 copy-done.1
  40.0 0.0 copy-done.2
  40.0 4.4 %shard_map.159 = (bf16[32,2,128,128]{3,2,1,0:T(8,128)(2,1)}, f32[64,256,32]{2,1,0:T(8,128)}) custom-call(f32[1024,128]{1,0:T(8,128)S(1)} %get-tuple-element.7.rr, f32[32,2,128,128]{3,2,1,0:T(8,128)S(1)} %get-tuple-element.8.mixed, f32[64,256,32]{2,1,0:T(8,128)S(1)} %get-tuple-element.9.gout, bf16[256,192]{1,0:T(8,128)(2,1)S(1)} %copy-done.2, ...), custom_call_target="tpu_custom_call" | custom-call | tf_op jit(solution)/shard_map/pallas_call | solution.py:470
Async XLA Ops:
  0.6 39.3 %copy-start = (bf16[256,512]{1,0:T(8,128)(2,1)S(1)}, bf16[256,512]{1,0:T(8,128)(2,1)}, u32[]{:S(2)}) copy-start(bf16[256,512]{1,0:T(8,128)(2,1)} %constant.29.clone.zl) | copy-start | bytes 786436
  0.6 39.3 %copy-start.1 = (bf16[256,512]{1,0:T(8,128)(2,1)S(1)}, bf16[256,512]{1,0:T(8,128)(2,1)}, u32[]{:S(2)}) copy-start(bf16[256,512]{1,0:T(8,128)(2,1)} %constant.28.clone.zh) | copy-start | bytes 786436
  0.7 39.3 %copy-start.2 = (bf16[256,192]{1,0:T(8,128)(2,1)S(1)}, bf16[256,192]{1,0:T(8,128)(2,1)}, u32[]{:S(2)}) copy-start(bf16[256,192]{1,0:T(8,128)(2,1)} %constant.27.clone.ys) | copy-start | bytes 294916
